TPU v7x, 32 devices: a whole 2x2x4 slice. The times are simulated.
32 devices in a mesh: lat: 2 (over x), lon: 16 (over z, y, core).
Axes of the slice: x: 2, y: 2, z: 4, core: 2. Of those that a mesh axis runs over, the one named last changes fastest.
Arguments:
- tracer: float32 [4, 512, 2048], P(None, 'lat', 'lon'), may hold values from -6 to 6
- wind_east: float32 [4, 512, 2048], P(None, 'lat', 'lon'), may hold values from -4 to 4
- wind_north: float32 [4, 512, 2048], P(None, 'lat', 'lon'), may hold values from -4 to 4
- kappa: float32 [4, 512, 2048], P(None, 'lat', 'lon'), may hold values from 0.25 to 4
- cutoff: int32 [128], replicated, may hold values from 64 to 511
- partner: int32 [2048], replicated, may hold values from 0 to 2047, as said below
Outputs:
- filtered: float32 [4, 512, 2048], P(None, 'lat', 'lon')
- balanced: float32 [4, 512, 2048], P(None, 'lat', 'lon')
Inputs may be any that keep to these rules, and one draw needn't show every extreme that they name: partner[j] = (j + 1024 + s_j) mod 2048 with each column's own shift s_j of 0 to 127; some column has s_j = 127.
All inputs are finite; a program needn't handle non-finite values.
Results may differ from a plain program's by a relative error of at most 0.00005.
Values sent between devices are 32-bit elements; how exact they have to be, the bound alone decides.
A program may use at most 64 MiB of HBM per device.

v0:
```python
import math

import jax
import jax.numpy as jnp
from jax import lax
from jax.sharding import PartitionSpec as P

KMAX = 512
SWEEPS = 4


COURANT = 0.4


def padded(cells, sides, width, closed):
    for axis, dim in sides:
        count = lax.axis_size(axis)
        ends = count if closed else count - 1
        head = lax.slice_in_dim(cells, 0, width, axis=dim)
        tail = lax.slice_in_dim(cells, cells.shape[dim] - width, cells.shape[dim], axis=dim)
        cells = jnp.concatenate(
            [
                lax.ppermute(tail, axis, [(i, (i + 1) % count) for i in range(ends)]),
                cells,
                lax.ppermute(head, axis, [((i + 1) % count, i) for i in range(ends)]),
            ],
            axis=dim,
        )
    return cells


def neighbours(field, partner):
    width = field.shape[2]
    lon_index = lax.axis_index("lon")
    lon_padded = padded(field, (("lon", 2),), 1, True)
    lat_padded = padded(field, (("lat", 1),), 1, False)
    edge_rows = jnp.stack([field[:, 0, :], field[:, -1, :]], axis=1)
    own_partner = lax.dynamic_slice_in_dim(partner, lon_index * width, width)
    whole_rows = lax.all_gather(edge_rows, "lon", axis=2, tiled=True)
    across = jnp.take(whole_rows, own_partner, axis=2)
    lat_index = lax.axis_index("lat")
    last_band = lax.axis_size("lat") - 1
    upper_row = jnp.where(lat_index == 0, across[:, 0, :], lat_padded[:, 0, :])
    lower_row = jnp.where(lat_index == last_band, across[:, 1, :], lat_padded[:, -1, :])
    upper = jnp.concatenate([upper_row[:, None, :], field[:, :-1, :]], axis=1)
    lower = jnp.concatenate([field[:, 1:, :], lower_row[:, None, :]], axis=1)
    western = lon_padded[:, :, :-2]
    eastern = lon_padded[:, :, 2:]
    return (western, eastern, upper, lower)


def tables(start, count, total, kmaximum):
    columns = start + jnp.arange(count, dtype=jnp.int32)
    waves = jnp.arange(kmaximum, dtype=jnp.int32)
    phase = columns[:, None] * waves[None, :] % total
    angle = phase.astype(jnp.float32) * (2.0 * math.pi / total)
    return (jnp.cos(angle), jnp.sin(angle))


def project(rows, start, total, kmaximum):
    cosine, sine = tables(start, rows.shape[1], total, kmaximum)
    cos_part = jnp.dot(
        rows, cosine, precision=lax.Precision.HIGHEST, preferred_element_type=jnp.float32
    )
    sin_part = jnp.dot(
        rows, sine, precision=lax.Precision.HIGHEST, preferred_element_type=jnp.float32
    )
    return (cos_part, sin_part)


def rebuild(cos_part, sin_part, limits, start, count, total):
    kmaximum = cos_part.shape[1]
    waves = jnp.arange(kmaximum, dtype=jnp.int32)
    weights = jnp.where(waves == 0, 1.0, 2.0).astype(jnp.float32) / total
    scaled = jnp.where(waves[None, :] <= limits[:, None], weights[None, :], 0.0)
    cosine, sine = tables(start, count, total, kmaximum)
    contract = (((1,), (1,)), ((), ()))
    first_term = lax.dot_general(
        cos_part * scaled,
        cosine,
        contract,
        precision=lax.Precision.HIGHEST,
        preferred_element_type=jnp.float32,
    )
    second_term = lax.dot_general(
        sin_part * scaled,
        sine,
        contract,
        precision=lax.Precision.HIGHEST,
        preferred_element_type=jnp.float32,
    )
    return first_term + second_term


def polar_filter(field, cutoff):
    levels, band_rows, width = field.shape
    pole_rows = cutoff.shape[0] // 2
    sectors = lax.axis_size("lon")
    total = width * sectors
    lon_index = lax.axis_index("lon")
    lat_index = lax.axis_index("lat")
    is_north = lat_index == 0
    is_south = lat_index == lax.axis_size("lat") - 1
    band = jnp.where(is_north, field[:, :pole_rows, :], field[:, band_rows - pole_rows :, :])
    band_limits = jnp.where(is_north, cutoff[:pole_rows], cutoff[pole_rows:])
    flat = band.reshape(levels * pole_rows, width)
    row_limits = jnp.tile(band_limits, levels)
    own_start = lon_index * width
    cos_add, sin_add = project(
        lax.all_gather(flat, "lon", axis=1, tiled=True), jnp.int32(0), total, KMAX
    )
    smooth = rebuild(cos_add, sin_add, row_limits, own_start, width, total)
    smooth = smooth.reshape(levels, pole_rows, width)
    top_rows = jnp.where(is_north, smooth, field[:, :pole_rows, :])
    bottom_rows = jnp.where(is_south, smooth, field[:, band_rows - pole_rows :, :])
    return jnp.concatenate(
        [top_rows, field[:, pole_rows : band_rows - pole_rows, :], bottom_rows], axis=1
    )


def per_device(tracer, wind_east, wind_north, kappa, cutoff, partner):
    western, eastern, upper, lower = neighbours(tracer, partner)
    advected = tracer - COURANT * 0.5 * (
        wind_east * (eastern - western) + wind_north * (lower - upper)
    )
    filtered = polar_filter(advected, cutoff)
    balanced = filtered
    for sweep_index in range(SWEEPS):
        western, eastern, upper, lower = neighbours(balanced, partner)
        balanced = (filtered + kappa * (western + eastern + upper + lower)) / (1.0 + 4.0 * kappa)
    return (filtered, balanced)


def solution(mesh):
    in_specs = (
        P(None, "lat", "lon"),
        P(None, "lat", "lon"),
        P(None, "lat", "lon"),
        P(None, "lat", "lon"),
        P(),
        P(),
    )
    out_specs = (P(None, "lat", "lon"), P(None, "lat", "lon"))
    return jax.shard_map(
        per_device, mesh=mesh, in_specs=in_specs, out_specs=out_specs, check_vma=False
    )
```

profile of v0, /device:TPU:0, one launch (start us, length us, event | category | flops | bytes accessed | tf_op | source)
XLA Modules:
  0.0 314.9 jit_solution(2903918422624642746)
XLA Ops:
  9.3 4.8 %collective-permute-start.3 = (f32[4,1,128]{2,1,0:T(1,128)S(1)}, f32[4,1,128]{2,1,0:T(1,128)S(1)}, u32[]{:S(2)}, u32[]{:S(2)}) collective-permute-start(f32[4,1,128]{2,1,0:T(1,128)S(1)} %get-tuple-element.39), channel_id=1, source_target_pairs={{0,16},{1,17},{2,18},{3,19},{4,20},{5,21},{6,22},{7,23},{8,24},{9,... | collective-permute-start | bytes 6152 | tf_op jit(solution)/shard_map/ppermute | solution.py:23
  16.5 4.6 %collective-permute-start = (f32[4,256,1]{2,1,0:T(8,128)}, f32[4,256,1]{2,1,0:T(8,128)S(1)}, u32[]{:S(2)}, u32[]{:S(2)}) collective-permute-start(f32[4,256,1]{2,1,0:T(8,128)} %get-tuple-element.41), channel_id=1, source_target_pairs={{1,0},{2,1},{3,2},{4,3},{5,4},{6,5},{7,6},{8,7},{9,8},{10,9},{11,1... | collective-permute-start | bytes 12296 | tf_op jit(solution)/shard_map/ppermute | solution.py:25
  22.9 21.6 %all_gather.18 = f32[4,2,2048]{2,0,1:T(4,128)S(1)} all-gather(f32[4,2,128]{2,0,1:T(4,128)S(1)} %pad_maximum_fusion.15), channel_id=1, replica_groups=mesh['lat'=2,'lon'=16] {'lon'}, dimensions={2}, use_global_device_ids=true | all-gather | bytes 69632 | tf_op jit(solution)/shard_map/all_gather | solution.py:39
  50.5 38.3 %all-gather.2.cloned.1.call-done = f32[256,2048]{1,0:T(8,128)} async-done(((f32[256,128]{1,0:T(8,128)}), f32[256,2048]{1,0:T(8,128)}) %all-gather.2.cloned.1.call-update) | async-done | bytes 2097168 | tf_op jit(solution)/shard_map/all_gather | solution.py:110
  88.9 21.2 %fusion.12 = f32[256,512]{1,0:T(8,128)S(1)} fusion(f32[256,2048]{1,0:T(8,128)} %all-gather.2.cloned.1.call-done, f32[512]{0:T(512)S(1)} %select_multiply_fusion, s32[256]{0:T(256)S(1)} %le.23), kind=kOutput, calls=%fused_computation.18 | convolution fusion | flops 3236298752 | bytes 2624512 | tf_op jit(solution)/shard_map/dot_general | solution.py:62
  111.7 19.7 %fusion.15 = f32[256,512]{1,0:T(8,128)S(1)} fusion(f32[256,2048]{1,0:T(8,128)S(1)} %copy-done.5, f32[512]{0:T(512)S(1)} %select_multiply_fusion, s32[256]{0:T(256)S(1)} %le.23), kind=kOutput, calls=%fused_computation.19 | convolution fusion | flops 3236298752 | bytes 2624512 | tf_op jit(solution)/shard_map/dot_general | solution.py:65
  135.3 3.4 %collective-permute-start.6 = (f32[4,1,128]{2,1,0:T(1,128)S(1)}, f32[4,1,128]{2,1,0:T(1,128)S(1)}, u32[]{:S(2)}, u32[]{:S(2)}) collective-permute-start(f32[4,1,128]{2,1,0:T(1,128)S(1)} %slice.260), channel_id=1, source_target_pairs={{0,16},{1,17},{2,18},{3,19},{4,20},{5,21},{6,22},{7,23},{8,24},{9,... | collective-permute-start | bytes 6152 | tf_op jit(solution)/shard_map/ppermute | solution.py:23
  140.0 19.5 %all_gather.20 = f32[4,2,2048]{2,0,1:T(4,128)S(1)} all-gather(f32[4,2,128]{2,0,1:T(4,128)S(1)} %pad_maximum_fusion.16), channel_id=1, replica_groups=mesh['lat'=2,'lon'=16] {'lon'}, dimensions={2}, use_global_device_ids=true | all-gather | bytes 69632 | tf_op jit(solution)/shard_map/all_gather | solution.py:39
  161.8 4.1 %collective-permute-start.5 = (f32[4,256,1]{2,1,0:T(8,128)}, f32[4,256,1]{2,1,0:T(8,128)S(1)}, u32[]{:S(2)}, u32[]{:S(2)}) collective-permute-start(f32[4,256,1]{2,1,0:T(8,128)} %get-tuple-element.36), channel_id=1, source_target_pairs={{1,0},{2,1},{3,2},{4,3},{5,4},{6,5},{7,6},{8,7},{9,8},{10,9},{11,1... | collective-permute-start | bytes 12296 | tf_op jit(solution)/shard_map/ppermute | solution.py:25
  165.9 7.2 %collective-permute-done.4 = f32[4,256,1]{2,1,0:T(8,128)S(1)} collective-permute-done((f32[4,256,1]{2,1,0:T(8,128)}, f32[4,256,1]{2,1,0:T(8,128)S(1)}, u32[]{:S(2)}, u32[]{:S(2)}) %collective-permute-start.4) | collective-permute-done | bytes 4128 | tf_op jit(solution)/shard_map/ppermute | solution.py:23
  175.9 4.5 %collective-permute-start.10 = (f32[4,1,128]{2,1,0:T(1,128)S(1)}, f32[4,1,128]{2,1,0:T(1,128)S(1)}, u32[]{:S(2)}, u32[]{:S(2)}) collective-permute-start(f32[4,1,128]{2,1,0:T(1,128)S(1)} %get-tuple-element.30), channel_id=1, source_target_pairs={{0,16},{1,17},{2,18},{3,19},{4,20},{5,21},{6,22},{7,23},{8,24},{9,... | collective-permute-start | bytes 6152 | tf_op jit(solution)/shard_map/ppermute | solution.py:23
  181.7 20.3 %all_gather.21 = f32[4,2,2048]{2,0,1:T(4,128)S(1)} all-gather(f32[4,2,128]{2,0,1:T(4,128)S(1)} %pad_maximum_fusion.17), channel_id=1, replica_groups=mesh['lat'=2,'lon'=16] {'lon'}, dimensions={2}, use_global_device_ids=true | all-gather | bytes 69632 | tf_op jit(solution)/shard_map/all_gather | solution.py:39
  204.4 2.3 gather_fusion.2
  207.2 4.1 %collective-permute-start.9 = (f32[4,256,1]{2,1,0:T(8,128)S(1)}, f32[4,256,1]{2,1,0:T(8,128)S(1)}, u32[]{:S(2)}, u32[]{:S(2)}) collective-permute-start(f32[4,256,1]{2,1,0:T(8,128)S(1)} %get-tuple-element.32), channel_id=1, source_target_pairs={{1,0},{2,1},{3,2},{4,3},{5,4},{6,5},{7,6},{8,7},{9,8},{10,9},{11,1... | collective-permute-start | bytes 12296 | tf_op jit(solution)/shard_map/ppermute | solution.py:25
  211.3 7.2 %collective-permute-done.8 = f32[4,256,1]{2,1,0:T(8,128)S(1)} collective-permute-done((f32[4,256,1]{2,1,0:T(8,128)}, f32[4,256,1]{2,1,0:T(8,128)S(1)}, u32[]{:S(2)}, u32[]{:S(2)}) %collective-permute-start.8) | collective-permute-done | bytes 4128 | tf_op jit(solution)/shard_map/ppermute | solution.py:23
  220.1 4.5 %collective-permute-start.14 = (f32[4,1,128]{2,1,0:T(1,128)S(1)}, f32[4,1,128]{2,1,0:T(1,128)S(1)}, u32[]{:S(2)}, u32[]{:S(2)}) collective-permute-start(f32[4,1,128]{2,1,0:T(1,128)S(1)} %get-tuple-element.24), channel_id=1, source_target_pairs={{0,16},{1,17},{2,18},{3,19},{4,20},{5,21},{6,22},{7,23},{8,24},{9,... | collective-permute-start | bytes 6152 | tf_op jit(solution)/shard_map/ppermute | solution.py:23
  225.9 20.3 %all_gather.22 = f32[4,2,2048]{2,0,1:T(4,128)S(1)} all-gather(f32[4,2,128]{2,0,1:T(4,128)S(1)} %pad_maximum_fusion.18), channel_id=1, replica_groups=mesh['lat'=2,'lon'=16] {'lon'}, dimensions={2}, use_global_device_ids=true | all-gather | bytes 69632 | tf_op jit(solution)/shard_map/all_gather | solution.py:39
  248.5 2.3 gather_fusion.3
  251.4 4.1 %collective-permute-start.13 = (f32[4,256,1]{2,1,0:T(8,128)S(1)}, f32[4,256,1]{2,1,0:T(8,128)S(1)}, u32[]{:S(2)}, u32[]{:S(2)}) collective-permute-start(f32[4,256,1]{2,1,0:T(8,128)S(1)} %get-tuple-element.26), channel_id=1, source_target_pairs={{1,0},{2,1},{3,2},{4,3},{5,4},{6,5},{7,6},{8,7},{9,8},{10,9},{11,1... | collective-permute-start | bytes 12296 | tf_op jit(solution)/shard_map/ppermute | solution.py:25
  255.5 7.2 %collective-permute-done.12 = f32[4,256,1]{2,1,0:T(8,128)S(1)} collective-permute-done((f32[4,256,1]{2,1,0:T(8,128)}, f32[4,256,1]{2,1,0:T(8,128)S(1)}, u32[]{:S(2)}, u32[]{:S(2)}) %collective-permute-start.12) | collective-permute-done | bytes 4128 | tf_op jit(solution)/shard_map/ppermute | solution.py:23
  264.2 4.5 %collective-permute-start.18 = (f32[4,1,128]{2,1,0:T(1,128)S(1)}, f32[4,1,128]{2,1,0:T(1,128)S(1)}, u32[]{:S(2)}, u32[]{:S(2)}) collective-permute-start(f32[4,1,128]{2,1,0:T(1,128)S(1)} %get-tuple-element.18), channel_id=1, source_target_pairs={{0,16},{1,17},{2,18},{3,19},{4,20},{5,21},{6,22},{7,23},{8,24},{9,... | collective-permute-start | bytes 6152 | tf_op jit(solution)/shard_map/ppermute | solution.py:23
  270.1 20.3 %all_gather.23 = f32[4,2,2048]{2,0,1:T(4,128)S(1)} all-gather(f32[4,2,128]{2,0,1:T(4,128)S(1)} %pad_maximum_fusion.19), channel_id=1, replica_groups=mesh['lat'=2,'lon'=16] {'lon'}, dimensions={2}, use_global_device_ids=true | all-gather | bytes 69632 | tf_op jit(solution)/shard_map/all_gather | solution.py:39
  295.5 4.1 %collective-permute-start.17 = (f32[4,256,1]{2,1,0:T(8,128)S(1)}, f32[4,256,1]{2,1,0:T(8,128)S(1)}, u32[]{:S(2)}, u32[]{:S(2)}) collective-permute-start(f32[4,256,1]{2,1,0:T(8,128)S(1)} %get-tuple-element.20), channel_id=1, source_target_pairs={{1,0},{2,1},{3,2},{4,3},{5,4},{6,5},{7,6},{8,7},{9,8},{10,9},{11,1... | collective-permute-start | bytes 12296 | tf_op jit(solution)/shard_map/ppermute | solution.py:25
  299.6 7.2 %collective-permute-done.16 = f32[4,256,1]{2,1,0:T(8,128)S(1)} collective-permute-done((f32[4,256,1]{2,1,0:T(8,128)}, f32[4,256,1]{2,1,0:T(8,128)S(1)}, u32[]{:S(2)}, u32[]{:S(2)}) %collective-permute-start.16) | collective-permute-done | bytes 4128 | tf_op jit(solution)/shard_map/ppermute | solution.py:23
  (102 shorter events, 43.1 us)
Async XLA Ops:
  7.2 13.9 %copy-start = (f32[4,256,128]{2,1,0:T(8,128)S(1)}, f32[4,256,128]{2,1,0:T(8,128)}, u32[]{:S(2)}) copy-start(f32[4,256,128]{2,1,0:T(8,128)} %param.8) | copy-start | bytes 1572868
  7.2 81.7 %all-gather.2.cloned.1.call-start = ((), (), s32[]{:S(2)}) async-start(), calls=%async_computation | async-start | bytes 2228224 | tf_op jit(solution)/shard_map/all_gather | solution.py:110
  8.0 38.5 %collective-permute-start.2 = (f32[4,1,128]{2,1,0:T(1,128)S(1)}, f32[4,1,128]{2,1,0:T(1,128)S(1)}, u32[]{:S(2)}, u32[]{:S(2)}) collective-permute-start(f32[4,1,128]{2,1,0:T(1,128)S(1)} %get-tuple-element.40), channel_id=1, source_target_pairs={{16,0},{17,1},{18,2},{19,3},{20,4},{21,5},{22,6},{23,7},{24,8},{25... | collective-permute-start | bytes 6152 | tf_op jit(solution)/shard_map/ppermute | solution.py:25
  9.3 37.2 %collective-permute-start.3 = (f32[4,1,128]{2,1,0:T(1,128)S(1)}, f32[4,1,128]{2,1,0:T(1,128)S(1)}, u32[]{:S(2)}, u32[]{:S(2)}) collective-permute-start(f32[4,1,128]{2,1,0:T(1,128)S(1)} %get-tuple-element.39), channel_id=1, source_target_pairs={{0,16},{1,17},{2,18},{3,19},{4,20},{5,21},{6,22},{7,23},{8,24},{9,... | collective-permute-start | bytes 6152 | tf_op jit(solution)/shard_map/ppermute | solution.py:23
  16.5 30.0 %collective-permute-start = (f32[4,256,1]{2,1,0:T(8,128)}, f32[4,256,1]{2,1,0:T(8,128)S(1)}, u32[]{:S(2)}, u32[]{:S(2)}) collective-permute-start(f32[4,256,1]{2,1,0:T(8,128)} %get-tuple-element.41), channel_id=1, source_target_pairs={{1,0},{2,1},{3,2},{4,3},{5,4},{6,5},{7,6},{8,7},{9,8},{10,9},{11,1... | collective-permute-start | bytes 12296 | tf_op jit(solution)/shard_map/ppermute | solution.py:25
  21.1 25.5 %collective-permute-start.1 = (f32[4,256,1]{2,1,0:T(8,128)}, f32[4,256,1]{2,1,0:T(8,128)}, u32[]{:S(2)}, u32[]{:S(2)}) collective-permute-start(f32[4,256,1]{2,1,0:T(8,128)} %get-tuple-element.42), channel_id=1, source_target_pairs={{0,1},{1,2},{2,3},{3,4},{4,5},{5,6},{6,7},{7,8},{8,9},{9,10},{10,1... | collective-permute-start | bytes 12296 | tf_op jit(solution)/shard_map/ppermute | solution.py:23
  88.8 22.8 %copy-start.5 = (f32[256,2048]{1,0:T(8,128)S(1)}, f32[256,2048]{1,0:T(8,128)}, u32[]{:S(2)}) copy-start(f32[256,2048]{1,0:T(8,128)} %all-gather.2.cloned.1.call-done) | copy-start | bytes 6291460
  134.2 38.9 %copy-start.2 = (f32[4,256,128]{2,1,0:T(8,128)S(1)}, f32[4,256,128]{2,1,0:T(8,128)}, u32[]{:S(2)}) copy-start(f32[4,256,128]{2,1,0:T(8,128)} %param.11) | copy-start | bytes 1572868
  135.3 30.6 %collective-permute-start.6 = (f32[4,1,128]{2,1,0:T(1,128)S(1)}, f32[4,1,128]{2,1,0:T(1,128)S(1)}, u32[]{:S(2)}, u32[]{:S(2)}) collective-permute-start(f32[4,1,128]{2,1,0:T(1,128)S(1)} %slice.260), channel_id=1, source_target_pairs={{0,16},{1,17},{2,18},{3,19},{4,20},{5,21},{6,22},{7,23},{8,24},{9,... | collective-permute-start | bytes 6152 | tf_op jit(solution)/shard_map/ppermute | solution.py:23
  138.7 27.2 %collective-permute-start.7 = (f32[4,1,128]{2,1,0:T(1,128)S(1)}, f32[4,1,128]{2,1,0:T(1,128)S(1)}, u32[]{:S(2)}, u32[]{:S(2)}) collective-permute-start(f32[4,1,128]{2,1,0:T(1,128)S(1)} %slice.259), channel_id=1, source_target_pairs={{16,0},{17,1},{18,2},{19,3},{20,4},{21,5},{22,6},{23,7},{24,8},{25... | collective-permute-start | bytes 6152 | tf_op jit(solution)/shard_map/ppermute | solution.py:25
  161.4 11.7 %collective-permute-start.4 = (f32[4,256,1]{2,1,0:T(8,128)}, f32[4,256,1]{2,1,0:T(8,128)S(1)}, u32[]{:S(2)}, u32[]{:S(2)}) collective-permute-start(f32[4,256,1]{2,1,0:T(8,128)} %get-tuple-element.35), channel_id=1, source_target_pairs={{0,1},{1,2},{2,3},{3,4},{4,5},{5,6},{6,7},{7,8},{8,9},{9,10},{10,1... | collective-permute-start | bytes 12296 | tf_op jit(solution)/shard_map/ppermute | solution.py:23
  161.8 11.3 %collective-permute-start.5 = (f32[4,256,1]{2,1,0:T(8,128)}, f32[4,256,1]{2,1,0:T(8,128)S(1)}, u32[]{:S(2)}, u32[]{:S(2)}) collective-permute-start(f32[4,256,1]{2,1,0:T(8,128)} %get-tuple-element.36), channel_id=1, source_target_pairs={{1,0},{2,1},{3,2},{4,3},{5,4},{6,5},{7,6},{8,7},{9,8},{10,9},{11,1... | collective-permute-start | bytes 12296 | tf_op jit(solution)/shard_map/ppermute | solution.py:25
  175.9 35.4 %collective-permute-start.10 = (f32[4,1,128]{2,1,0:T(1,128)S(1)}, f32[4,1,128]{2,1,0:T(1,128)S(1)}, u32[]{:S(2)}, u32[]{:S(2)}) collective-permute-start(f32[4,1,128]{2,1,0:T(1,128)S(1)} %get-tuple-element.30), channel_id=1, source_target_pairs={{0,16},{1,17},{2,18},{3,19},{4,20},{5,21},{6,22},{7,23},{8,24},{9,... | collective-permute-start | bytes 6152 | tf_op jit(solution)/shard_map/ppermute | solution.py:23
  180.4 30.9 %collective-permute-start.11 = (f32[4,1,128]{2,1,0:T(1,128)S(1)}, f32[4,1,128]{2,1,0:T(1,128)S(1)}, u32[]{:S(2)}, u32[]{:S(2)}) collective-permute-start(f32[4,1,128]{2,1,0:T(1,128)S(1)} %get-tuple-element.29), channel_id=1, source_target_pairs={{16,0},{17,1},{18,2},{19,3},{20,4},{21,5},{22,6},{23,7},{24,8},{25... | collective-permute-start | bytes 6152 | tf_op jit(solution)/shard_map/ppermute | solution.py:25
  206.8 11.7 %collective-permute-start.8 = (f32[4,256,1]{2,1,0:T(8,128)}, f32[4,256,1]{2,1,0:T(8,128)S(1)}, u32[]{:S(2)}, u32[]{:S(2)}) collective-permute-start(f32[4,256,1]{2,1,0:T(8,128)} %get-tuple-element.31), channel_id=1, source_target_pairs={{0,1},{1,2},{2,3},{3,4},{4,5},{5,6},{6,7},{7,8},{8,9},{9,10},{10,1... | collective-permute-start | bytes 12296 | tf_op jit(solution)/shard_map/ppermute | solution.py:23
  207.2 11.3 %collective-permute-start.9 = (f32[4,256,1]{2,1,0:T(8,128)S(1)}, f32[4,256,1]{2,1,0:T(8,128)S(1)}, u32[]{:S(2)}, u32[]{:S(2)}) collective-permute-start(f32[4,256,1]{2,1,0:T(8,128)S(1)} %get-tuple-element.32), channel_id=1, source_target_pairs={{1,0},{2,1},{3,2},{4,3},{5,4},{6,5},{7,6},{8,7},{9,8},{10,9},{11,1... | collective-permute-start | bytes 12296 | tf_op jit(solution)/shard_map/ppermute | solution.py:25
  220.1 35.4 %collective-permute-start.14 = (f32[4,1,128]{2,1,0:T(1,128)S(1)}, f32[4,1,128]{2,1,0:T(1,128)S(1)}, u32[]{:S(2)}, u32[]{:S(2)}) collective-permute-start(f32[4,1,128]{2,1,0:T(1,128)S(1)} %get-tuple-element.24), channel_id=1, source_target_pairs={{0,16},{1,17},{2,18},{3,19},{4,20},{5,21},{6,22},{7,23},{8,24},{9,... | collective-permute-start | bytes 6152 | tf_op jit(solution)/shard_map/ppermute | solution.py:23
  224.6 30.9 %collective-permute-start.15 = (f32[4,1,128]{2,1,0:T(1,128)S(1)}, f32[4,1,128]{2,1,0:T(1,128)S(1)}, u32[]{:S(2)}, u32[]{:S(2)}) collective-permute-start(f32[4,1,128]{2,1,0:T(1,128)S(1)} %get-tuple-element.23), channel_id=1, source_target_pairs={{16,0},{17,1},{18,2},{19,3},{20,4},{21,5},{22,6},{23,7},{24,8},{25... | collective-permute-start | bytes 6152 | tf_op jit(solution)/shard_map/ppermute | solution.py:25
  251.0 11.7 %collective-permute-start.12 = (f32[4,256,1]{2,1,0:T(8,128)}, f32[4,256,1]{2,1,0:T(8,128)S(1)}, u32[]{:S(2)}, u32[]{:S(2)}) collective-permute-start(f32[4,256,1]{2,1,0:T(8,128)} %get-tuple-element.25), channel_id=1, source_target_pairs={{0,1},{1,2},{2,3},{3,4},{4,5},{5,6},{6,7},{7,8},{8,9},{9,10},{10,1... | collective-permute-start | bytes 12296 | tf_op jit(solution)/shard_map/ppermute | solution.py:23
  251.4 11.3 %collective-permute-start.13 = (f32[4,256,1]{2,1,0:T(8,128)S(1)}, f32[4,256,1]{2,1,0:T(8,128)S(1)}, u32[]{:S(2)}, u32[]{:S(2)}) collective-permute-start(f32[4,256,1]{2,1,0:T(8,128)S(1)} %get-tuple-element.26), channel_id=1, source_target_pairs={{1,0},{2,1},{3,2},{4,3},{5,4},{6,5},{7,6},{8,7},{9,8},{10,9},{11,1... | collective-permute-start | bytes 12296 | tf_op jit(solution)/shard_map/ppermute | solution.py:25
  264.2 35.4 %collective-permute-start.18 = (f32[4,1,128]{2,1,0:T(1,128)S(1)}, f32[4,1,128]{2,1,0:T(1,128)S(1)}, u32[]{:S(2)}, u32[]{:S(2)}) collective-permute-start(f32[4,1,128]{2,1,0:T(1,128)S(1)} %get-tuple-element.18), channel_id=1, source_target_pairs={{0,16},{1,17},{2,18},{3,19},{4,20},{5,21},{6,22},{7,23},{8,24},{9,... | collective-permute-start | bytes 6152 | tf_op jit(solution)/shard_map/ppermute | solution.py:23
  268.8 30.9 %collective-permute-start.19 = (f32[4,1,128]{2,1,0:T(1,128)S(1)}, f32[4,1,128]{2,1,0:T(1,128)S(1)}, u32[]{:S(2)}, u32[]{:S(2)}) collective-permute-start(f32[4,1,128]{2,1,0:T(1,128)S(1)} %get-tuple-element.17), channel_id=1, source_target_pairs={{16,0},{17,1},{18,2},{19,3},{20,4},{21,5},{22,6},{23,7},{24,8},{25... | collective-permute-start | bytes 6152 | tf_op jit(solution)/shard_map/ppermute | solution.py:25
  295.2 11.7 %collective-permute-start.16 = (f32[4,256,1]{2,1,0:T(8,128)}, f32[4,256,1]{2,1,0:T(8,128)S(1)}, u32[]{:S(2)}, u32[]{:S(2)}) collective-permute-start(f32[4,256,1]{2,1,0:T(8,128)} %get-tuple-element.19), channel_id=1, source_target_pairs={{0,1},{1,2},{2,3},{3,4},{4,5},{5,6},{6,7},{7,8},{8,9},{9,10},{10,1... | collective-permute-start | bytes 12296 | tf_op jit(solution)/shard_map/ppermute | solution.py:23
  295.5 11.3 %collective-permute-start.17 = (f32[4,256,1]{2,1,0:T(8,128)S(1)}, f32[4,256,1]{2,1,0:T(8,128)S(1)}, u32[]{:S(2)}, u32[]{:S(2)}) collective-permute-start(f32[4,256,1]{2,1,0:T(8,128)S(1)} %get-tuple-element.20), channel_id=1, source_target_pairs={{1,0},{2,1},{3,2},{4,3},{5,4},{6,5},{7,6},{8,7},{9,8},{10,9},{11,1... | collective-permute-start | bytes 12296 | tf_op jit(solution)/shard_map/ppermute | solution.py:25
  (3 other events, 10.8 us)
Sparse Core Ops, SparseCore 0:
  50.5 38.3 all-gather.1
where the time goes:
time: 318 us; the launch traced here: 315 us
  blocking collectives  102 us (32%)
  waiting for transfers between devices  67 us (21%)
  starting transfers between devices  50.8 us (16%)
  matrix products  44 us (14%)
  local copies, waits for them, and re-layouts  28.6 us (9%)
  between operations  14.4 us (5%)
  other arithmetic  8.01 us (3%)
    all_gather x5, blocking collectives, neighbours(): whole_rows = lax.all_gather(edge_rows, 'lon', axis=2, tiled=True)  102 us
    all_gather x1, waiting for transfers between devices, polar_filter(): lax.all_gather(flat, 'lon', axis=1, tiled=True)  38.3 us
    ppermute x10, waiting for transfers between devices, padded(): lax.ppermute(tail, axis, [(i, (i + 1) % count) for i in range(ends)])  28.7 us
    ppermute x10, starting transfers between devices, padded(): lax.ppermute(head, axis, [((i + 1) % count, i) for i in range(ends)])  27.4 us
    ppermute x10, starting transfers between devices, padded(): lax.ppermute(tail, axis, [(i, (i + 1) % count) for i in range(ends)])  23.3 us
    dot_general x1, matrix products, project(): jnp.dot(rows, cosine, precision=lax.Precision.HIGHEST, preferred_element_...  21.2 us
    dot_general x1, matrix products, project(): jnp.dot(rows, sine, precision=lax.Precision.HIGHEST, preferred_element_ty...  19.7 us
    all_gather x5, local copies, waits for them, and re-layouts, neighbours(): whole_rows = lax.all_gather(edge_rows, 'lon', axis=2, tiled=True)  9.14 us
  transfers between devices with their start and end apart: 21, of which 5 were waited for; matrix products, arithmetic and copies ran while one was open for 7% of the time, Pallas kernels for 0%

commit v1 on v0

v1 whole, which is shorter than its diff:
```python
import functools
import math

import jax
import jax.numpy as jnp
import numpy as np
from jax import lax
from jax.experimental import pallas as pl
from jax.experimental.pallas import tpu as pltpu
from jax.sharding import PartitionSpec as P

KMAX = 512
SWEEPS = 4
COURANT = 0.4
HIGHEST = lax.Precision.HIGHEST


def tables(sectors, width):
    total = sectors * width
    half = sectors // 2
    m = np.arange(width)
    theta = 2.0 * np.pi * (np.outer(np.arange(half + 1), m) % total) / total
    kept = 2 * KMAX // sectors
    k2 = np.arange(kept) - kept // 2
    phase = 2.0 * np.pi * (np.outer(m, k2) % width) / width
    c, s = np.cos(phase), np.sin(phase)
    forward = np.block([[c, -s], [s, c]])
    inverse = np.block([[c.T, s.T], [-s.T, c.T]]) / total
    return [a.astype(np.float32) for a in (np.cos(theta), np.sin(theta), forward, inverse)]


def weighted(terms):
    total = None
    for factor, value in terms:
        if abs(factor) < 1e-12:
            continue
        part = value if abs(factor - 1.0) < 1e-12 else value * np.float32(factor)
        total = part if total is None else total + part
    return total


def kernel(
    sectors, bands,
    tracer, wind_east, wind_north, kappa, cutoff, partner, tw_cos, tw_sin, fwd, inv,
    filtered, balanced,
    col_send, col_recv, edge_send, edge_recv, spread, send_b, recv_b, coupling, scaled, ping, pong,
    halo_ss, halo_rs, a_ss, a_rs, b_ss, b_rs,
):
    lev, rows, width = tracer.shape
    pole = cutoff.shape[1] // 2
    share = lev * pole // sectors
    slices = sectors // lev
    half = sectors // 2
    groups = lev * rows // 8
    per = rows // 8
    lat = lax.axis_index("lat")
    lon = lax.axis_index("lon")

    def sector(offset):
        return lax.rem(lon + (offset % sectors), sectors)

    def band(offset):
        return lax.rem(lat + (offset % bands), bands)

    barrier = pltpu.get_barrier_semaphore()
    for t in range(1, sectors):
        pl.semaphore_signal(barrier, inc=1, device_id=(lat, sector(t)), device_id_type=pl.DeviceIdType.MESH)
    for t in (1, -1):
        pl.semaphore_signal(barrier, inc=1, device_id=(band(t), lon), device_id_type=pl.DeviceIdType.MESH)
    pl.semaphore_wait(barrier, sectors + 1)

    lane2 = lax.broadcasted_iota(jnp.int32, (rows, width), 1)
    row2 = lax.broadcasted_iota(jnp.int32, (rows, width), 0)
    diagonal = lax.broadcasted_iota(jnp.int32, (groups, 8, width), 0) == lax.broadcasted_iota(
        jnp.int32, (groups, 8, width), 2
    )
    reach = partner[pl.ds(lon, 1), :] - sector(half) * width
    reach = jnp.where(reach < 0, reach + sectors * width, reach)
    pick = jnp.where(
        lax.broadcasted_iota(jnp.int32, (2 * width, width), 0) == reach, 1.0, 0.0
    ).astype(jnp.float32)

    def post(turn, field):
        whole = field[...].reshape(groups, 8, width)
        col_send[turn, 0] = jnp.sum(jnp.where(diagonal, whole[:, :, width - 1 : width], 0.0), axis=0)
        col_send[turn, 1] = jnp.sum(jnp.where(diagonal, whole[:, :, 0:1], 0.0), axis=0)
        for l in range(lev):
            edge_send[turn, l : l + 1, :] = field[l, 0:1, :]
            edge_send[turn, lev + l : lev + l + 1, :] = field[l, rows - 1 : rows, :]
        plan = [
            (edge_send.at[turn], edge_recv.at[turn, 0], (lat, sector(-half))),
            (edge_send.at[turn], edge_recv.at[turn, 1], (lat, sector(-half - 1))),
            (edge_send.at[turn], edge_recv.at[turn, 2], (band(1), lon)),
            (edge_send.at[turn], edge_recv.at[turn, 3], (band(-1), lon)),
            (col_send.at[turn, 0], col_recv.at[turn, 0], (lat, sector(1))),
            (col_send.at[turn, 1], col_recv.at[turn, 1], (lat, sector(-1))),
        ]
        copies = []
        for i, (src, dst, device) in enumerate(plan):
            copy = pltpu.make_async_remote_copy(
                src_ref=src, dst_ref=dst, send_sem=halo_ss.at[turn, i], recv_sem=halo_rs.at[turn, i],
                device_id=device, device_id_type=pl.DeviceIdType.MESH,
            )
            copy.start()
            copies.append(copy)
        return copies

    def sides(turn):
        across = jnp.dot(
            jnp.concatenate([edge_recv[turn, 0], edge_recv[turn, 1]], axis=1), pick,
            precision=HIGHEST, preferred_element_type=jnp.float32,
        )
        top = jnp.where(lat == 0, across[:lev], edge_recv[turn, 2, lev:])
        bottom = jnp.where(lat == bands - 1, across[lev:], edge_recv[turn, 3, :lev])
        west = jnp.sum(jnp.where(diagonal, col_recv[turn, 0][None], 0.0), axis=2, keepdims=True)
        east = jnp.sum(jnp.where(diagonal, col_recv[turn, 1][None], 0.0), axis=2, keepdims=True)
        return top, bottom, west, east

    def around(field, l, edges):
        top, bottom, west, east = edges
        x = field[l]
        w = jnp.broadcast_to(west[per * l : per * (l + 1)], (per, 8, width)).reshape(rows, width)
        e = jnp.broadcast_to(east[per * l : per * (l + 1)], (per, 8, width)).reshape(rows, width)
        return (
            jnp.where(lane2 == 0, w, pltpu.roll(x, 1, 1)),
            jnp.where(lane2 == width - 1, e, pltpu.roll(x, width - 1, 1)),
            jnp.where(row2 == 0, top[l : l + 1], pltpu.roll(x, 1, 0)),
            jnp.where(row2 == rows - 1, bottom[l : l + 1], pltpu.roll(x, rows - 1, 0)),
        )

    copies = post(0, tracer)
    for l in range(lev):
        coupling[l] = kappa[l] / (1.0 + 4.0 * kappa[l])
    for copy in copies:
        copy.wait()
    edges = sides(0)
    for l in range(lev):
        w, e, u, d = around(tracer, l, edges)
        filtered[l] = tracer[l] - COURANT * 0.5 * (wind_east[l] * (e - w) + wind_north[l] * (d - u))

    base = jnp.where(lat == bands - 1, rows - pole, 0)

    def part(device):
        return lax.div(device, slices), pl.ds(pl.multiple_of(base + lax.rem(device, slices) * share, 8), share)

    copies = []
    for t in range(1, sectors):
        level, span = part(sector(t))
        copy = pltpu.make_async_remote_copy(
            src_ref=filtered.at[level, span, :], dst_ref=spread.at[lon],
            send_sem=a_ss.at[t], recv_sem=a_rs.at[t],
            device_id=(lat, sector(t)), device_id_type=pl.DeviceIdType.MESH,
        )
        copy.start()
        copies.append(copy)
    level, span = part(lon)
    spread[lon] = filtered[level, span, :]

    first = jnp.where(lat == bands - 1, pole, 0) + lax.rem(lon, slices) * share
    spot = lax.broadcasted_iota(jnp.int32, (share, 2 * pole), 0) + first
    limit = jnp.sum(
        jnp.where(
            lax.broadcasted_iota(jnp.int32, (share, 2 * pole), 1) == spot,
            cutoff[...].astype(jnp.float32), 0.0,
        ),
        axis=1, keepdims=True,
    )
    kept = 2 * KMAX // sectors
    slot = lax.broadcasted_iota(jnp.int32, (share, 2 * kept), 1)
    wave = sectors * (jnp.where(slot < kept, slot, slot - kept) - kept // 2)
    for copy in copies:
        copy.wait()

    def circle(d, k):
        angle = 2.0 * math.pi * ((d * k) % sectors) / sectors
        return math.cos(angle), math.sin(angle)

    even = [spread[0]] + [spread[d] + spread[sectors - d] for d in range(1, half)] + [spread[half]]
    odd = [None] + [spread[d] - spread[sectors - d] for d in range(1, half)]
    blocks = []
    for k in range(half + 1):
        c, s = tw_cos[k : k + 1, :], tw_sin[k : k + 1, :]
        re = weighted([(circle(d, k)[0], even[d]) for d in range(half + 1)])
        im = weighted([(-circle(d, k)[1], odd[d]) for d in range(1, half)])
        if im is None:
            blocks.append(jnp.concatenate([re * c, -(re * s)], axis=1))
        else:
            blocks.append(jnp.concatenate([re * c + im * s, im * c - re * s], axis=1))
    spectrum = jnp.dot(
        jnp.concatenate(blocks, axis=0), fwd[...], precision=HIGHEST, preferred_element_type=jnp.float32
    )
    keep = jnp.concatenate(
        [jnp.where(jnp.abs(wave + k).astype(jnp.float32) <= limit, 1.0, 0.0) for k in range(half + 1)], axis=0
    )
    back = jnp.dot(
        jnp.where(keep > 0.0, spectrum, 0.0), inv[...], precision=HIGHEST, preferred_element_type=jnp.float32
    )
    real, imag = [], []
    for k in range(half + 1):
        c, s = tw_cos[k : k + 1, :], tw_sin[k : k + 1, :]
        zr = back[k * share : (k + 1) * share, :width]
        zi = back[k * share : (k + 1) * share, width:]
        twice = 1.0 if k in (0, half) else 2.0
        real.append((zr * c - zi * s) * twice)
        imag.append((zr * s + zi * c) * twice)
    for d in range(half + 1):
        p = weighted([(circle(d, k)[0], real[k]) for k in range(half + 1)])
        q = weighted([(circle(d, k)[1], imag[k]) for k in range(1, half)])
        if q is None:
            send_b[d] = p
        else:
            send_b[d] = p - q
            send_b[sectors - d] = p + q

    copies = []
    for t in range(1, sectors):
        copy = pltpu.make_async_remote_copy(
            src_ref=send_b.at[sector(t)], dst_ref=recv_b.at[lon],
            send_sem=b_ss.at[t], recv_sem=b_rs.at[t],
            device_id=(lat, sector(t)), device_id_type=pl.DeviceIdType.MESH,
        )
        copy.start()
        copies.append(copy)
    recv_b[lon] = send_b[lon]
    for copy in copies:
        copy.wait()

    def restore(start):
        for l in range(lev):
            for q in range(slices):
                filtered[l, start + q * share : start + (q + 1) * share, :] = recv_b[l * slices + q]

    @pl.when(lat == 0)
    def _():
        restore(0)

    @pl.when(lat == bands - 1)
    def _():
        restore(rows - pole)

    chain = [filtered, ping, pong, ping, balanced]
    for sweep in range(SWEEPS):
        source, target = chain[sweep], chain[sweep + 1]
        copies = post(1 + sweep, source)
        if sweep == 0:
            for l in range(lev):
                scaled[l] = filtered[l] / (1.0 + 4.0 * kappa[l])
        for copy in copies:
            copy.wait()
        edges = sides(1 + sweep)
        for l in range(lev):
            w, e, u, d = around(source, l, edges)
            target[l] = scaled[l] + coupling[l] * (w + e + u + d)


def solution(mesh):
    sectors, bands = mesh.shape["lon"], mesh.shape["lat"]

    def per_device(tracer, wind_east, wind_north, kappa, cutoff, partner):
        lev, rows, width = tracer.shape
        share = lev * (cutoff.shape[0] // 2) // sectors
        turns = SWEEPS + 1
        block = pltpu.VMEM((lev, rows, width), jnp.float32)
        vmem = pl.BlockSpec(memory_space=pltpu.VMEM)
        return pl.pallas_call(
            functools.partial(kernel, sectors, bands),
            out_shape=[jax.ShapeDtypeStruct(tracer.shape, jnp.float32)] * 2,
            in_specs=[vmem] * 10,
            out_specs=[vmem] * 2,
            scratch_shapes=[
                pltpu.VMEM((turns, 2, 8, width), jnp.float32),
                pltpu.VMEM((turns, 2, 8, width), jnp.float32),
                pltpu.VMEM((turns, 2 * lev, width), jnp.float32),
                pltpu.VMEM((turns, 4, 2 * lev, width), jnp.float32),
                pltpu.VMEM((sectors, share, width), jnp.float32),
                pltpu.VMEM((sectors, share, width), jnp.float32),
                pltpu.VMEM((sectors, share, width), jnp.float32),
                block, block, block, block,
                pltpu.SemaphoreType.DMA((turns, 6)),
                pltpu.SemaphoreType.DMA((turns, 6)),
                pltpu.SemaphoreType.DMA((sectors,)),
                pltpu.SemaphoreType.DMA((sectors,)),
                pltpu.SemaphoreType.DMA((sectors,)),
                pltpu.SemaphoreType.DMA((sectors,)),
            ],
            compiler_params=pltpu.CompilerParams(
                collective_id=0, has_side_effects=True, vmem_limit_bytes=32 * 1024 * 1024
            ),
        )(
            tracer, wind_east, wind_north, kappa,
            cutoff.reshape(1, -1), partner.reshape(sectors, width),
            *tables(sectors, width),
        )

    spec = P(None, "lat", "lon")
    return jax.shard_map(
        per_device, mesh=mesh, in_specs=(spec, spec, spec, spec, P(), P()), out_specs=(spec, spec),
        check_vma=False,
    )
```

time: 318 us -> 51.3 us (0.16)
  blocking collectives: 102 us -> 0 us
  waiting for transfers between devices: 67 us -> 0 us
  starting transfers between devices: 50.8 us -> 0 us
  matrix products: 44 us -> 0 us
  Pallas kernels: 0 us -> 39.9 us
  local copies, waits for them, and re-layouts: 28.6 us -> 10.3 us
  between operations: 14.4 us -> 0.66 us
  other arithmetic: 8.01 us -> 0 us
    all_gather x5 -> x0, blocking collectives: 102 us -> none  [neighbours(): whole_rows = lax.all_gather(edge_rows, 'lon', axis=2, tiled=True)]
    ppermute x20 -> x0, starting transfers between devices: 50.8 us -> none  [the longest x10 27.4 us: padded(): lax.ppermute(head, axis, [((i + 1) % count, i) for i in range(ends)])]
    dot_general x4 -> x0, matrix products: 44 us -> none  [the longest x1 21.2 us: project(): jnp.dot(rows, cosine, precision=lax.Precision.HIGHEST, preferred_element_...]
    pallas_call x0 -> x1, Pallas kernels: none -> 39.9 us  [per_device(): pl.pallas_call(functools.partial(kernel, sectors, bands), out_shape=[jax....]
    all_gather x1 -> x0, waiting for transfers between devices: 38.3 us -> none  [polar_filter(): lax.all_gather(flat, 'lon', axis=1, tiled=True)]
    ppermute x20 -> x0, waiting for transfers between devices: 28.7 us -> none  [the longest x10 28.7 us: padded(): lax.ppermute(tail, axis, [(i, (i + 1) % count) for i in range(ends)])]
    slice x17 -> x0, local copies, waits for them, and re-layouts: 9.67 us -> none  [the longest x4 4.14 us: padded(): lax.slice_in_dim(cells, cells.shape[dim] - width, cells.shape[dim], axis=...]
    unnamed x12 -> x22, local copies, waits for them, and re-layouts: 0.8 us -> 10.3 us
  transfers between devices with their start and end apart: 21 -> 0, of which waited for: 5 -> 0; matrix products, arithmetic and copies ran while one was open for 7% -> 0% of each run, Pallas kernels for 0% -> 0%
where the time goes in v1:
time: 51.3 us; the launch traced here: 50.9 us
  Pallas kernels  39.9 us (78%)
  local copies, waits for them, and re-layouts  10.3 us (20%)
  between operations  0.66 us (1%)
    pallas_call x1, Pallas kernels, per_device(): pl.pallas_call(functools.partial(kernel, sectors, bands), out_shape=[jax....  39.9 us
    unnamed x22, local copies, waits for them, and re-layouts  10.3 us

profile of v1, /device:TPU:0, one launch (start us, length us, event | category | flops | bytes accessed | tf_op | source)
XLA Modules:
  0.0 50.9 jit_solution(12147793045787963919)
XLA Ops:
  0.6 0.0 copy-start.9
  0.6 0.6 %copy-done.9 = s32[128]{0:T(128)S(1)} copy-done((s32[128]{0:T(128)S(1)}, s32[128]{0:T(128)}, u32[]{:S(2)}) %copy-start.9) | copy-done | bytes 536
  1.3 0.0 copy-start
  1.3 1.0 %copy-done = f32[4,256,128]{2,1,0:T(8,128)S(1)} copy-done((f32[4,256,128]{2,1,0:T(8,128)S(1)}, f32[4,256,128]{2,1,0:T(8,128)}, u32[]{:S(2)}) %copy-start) | copy-done | bytes 524312
  2.3 0.0 copy-start.1
  2.3 1.0 %copy-done.1 = f32[4,256,128]{2,1,0:T(8,128)S(1)} copy-done((f32[4,256,128]{2,1,0:T(8,128)S(1)}, f32[4,256,128]{2,1,0:T(8,128)}, u32[]{:S(2)}) %copy-start.1) | copy-done | bytes 524312
  3.4 0.0 copy-start.2
  3.4 1.0 %copy-done.2 = f32[4,256,128]{2,1,0:T(8,128)S(1)} copy-done((f32[4,256,128]{2,1,0:T(8,128)S(1)}, f32[4,256,128]{2,1,0:T(8,128)}, u32[]{:S(2)}) %copy-start.2) | copy-done | bytes 524312
  4.4 0.0 copy-start.3
  4.4 1.0 %copy-done.3 = f32[4,256,128]{2,1,0:T(8,128)S(1)} copy-done((f32[4,256,128]{2,1,0:T(8,128)S(1)}, f32[4,256,128]{2,1,0:T(8,128)}, u32[]{:S(2)}) %copy-start.3) | copy-done | bytes 524312
  5.5 0.0 copy-start.4
  5.5 0.9 %copy-done.4 = f32[128,256]{1,0:T(8,128)S(1)} copy-done((f32[128,256]{1,0:T(8,128)S(1)}, f32[128,256]{1,0:T(8,128)}, u32[]{:S(2)}) %copy-start.4) | copy-done | bytes 131096
  6.4 0.0 copy-start.5
  6.4 0.9 %copy-done.5 = f32[256,128]{1,0:T(8,128)S(1)} copy-done((f32[256,128]{1,0:T(8,128)S(1)}, f32[256,128]{1,0:T(8,128)}, u32[]{:S(2)}) %copy-start.5) | copy-done | bytes 131096
  7.3 0.0 copy-start.6
  7.3 0.7 %copy-done.6 = s32[2048]{0:T(1024)S(1)} copy-done((s32[2048]{0:T(1024)S(1)}, s32[2048]{0:T(1024)}, u32[]{:S(2)}) %copy-start.6) | copy-done | bytes 8216
  8.0 0.0 copy-start.7
  8.0 0.7 %copy-done.7 = f32[9,128]{1,0:T(8,128)S(1)} copy-done((f32[9,128]{1,0:T(8,128)S(1)}, f32[9,128]{1,0:T(8,128)}, u32[]{:S(2)}) %copy-start.7) | copy-done | bytes 4632
  8.7 0.0 copy-start.8
  8.7 0.7 %copy-done.8 = f32[9,128]{1,0:T(8,128)S(1)} copy-done((f32[9,128]{1,0:T(8,128)S(1)}, f32[9,128]{1,0:T(8,128)}, u32[]{:S(2)}) %copy-start.8) | copy-done | bytes 4632
  9.4 39.9 %shard_map.113 = (f32[4,256,128]{2,1,0:T(8,128)S(1)}, f32[4,256,128]{2,1,0:T(8,128)S(1)}) custom-call(f32[4,256,128]{2,1,0:T(8,128)S(1)} %copy-done, f32[4,256,128]{2,1,0:T(8,128)S(1)} %copy-done.1, f32[4,256,128]{2,1,0:T(8,128)S(1)} %copy-done.2, f32[4,256,128]{2,1,0:T(8,128)S(1)} %copy-done.3, s32[1,128]{1,0:T(1,128)S(1)} %bitcast.3, ...), custom_call_target="tpu_custom_call" | custom-call | tf_op jit(solution)/shard_map/pallas_call | solution.py:265
  49.3 0.8 %copy.14 = f32[4,256,128]{2,1,0:T(8,128)} copy(f32[4,256,128]{2,1,0:T(8,128)S(1)} %get-tuple-element.4) | data formatting | bytes 1048576
  50.1 0.8 %copy.15 = f32[4,256,128]{2,1,0:T(8,128)} copy(f32[4,256,128]{2,1,0:T(8,128)S(1)} %get-tuple-element.5) | data formatting | bytes 1048576
Async XLA Ops:
  0.6 0.7 %copy-start.9 = (s32[128]{0:T(128)S(1)}, s32[128]{0:T(128)}, u32[]{:S(2)}) copy-start(s32[128]{0:T(128)} %param.14) | copy-start | bytes 1540
  1.3 1.0 %copy-start = (f32[4,256,128]{2,1,0:T(8,128)S(1)}, f32[4,256,128]{2,1,0:T(8,128)}, u32[]{:S(2)}) copy-start(f32[4,256,128]{2,1,0:T(8,128)} %tracer.1) | copy-start | bytes 1572868
  2.3 1.0 %copy-start.1 = (f32[4,256,128]{2,1,0:T(8,128)S(1)}, f32[4,256,128]{2,1,0:T(8,128)}, u32[]{:S(2)}) copy-start(f32[4,256,128]{2,1,0:T(8,128)} %wind_east.1) | copy-start | bytes 1572868
  3.4 1.0 %copy-start.2 = (f32[4,256,128]{2,1,0:T(8,128)S(1)}, f32[4,256,128]{2,1,0:T(8,128)}, u32[]{:S(2)}) copy-start(f32[4,256,128]{2,1,0:T(8,128)} %wind_north.1) | copy-start | bytes 1572868
  4.4 1.0 %copy-start.3 = (f32[4,256,128]{2,1,0:T(8,128)S(1)}, f32[4,256,128]{2,1,0:T(8,128)}, u32[]{:S(2)}) copy-start(f32[4,256,128]{2,1,0:T(8,128)} %kappa.1) | copy-start | bytes 1572868
  5.5 0.9 %copy-start.4 = (f32[128,256]{1,0:T(8,128)S(1)}, f32[128,256]{1,0:T(8,128)}, u32[]{:S(2)}) copy-start(f32[128,256]{1,0:T(8,128)} %constant.11.clone.inv) | copy-start | bytes 393220
  6.4 0.9 %copy-start.5 = (f32[256,128]{1,0:T(8,128)S(1)}, f32[256,128]{1,0:T(8,128)}, u32[]{:S(2)}) copy-start(f32[256,128]{1,0:T(8,128)} %constant.10.clone.fwd) | copy-start | bytes 393220
  7.3 0.7 %copy-start.6 = (s32[2048]{0:T(1024)S(1)}, s32[2048]{0:T(1024)}, u32[]{:S(2)}) copy-start(s32[2048]{0:T(1024)} %param.15) | copy-start | bytes 24580
  8.0 0.7 %copy-start.7 = (f32[9,128]{1,0:T(8,128)S(1)}, f32[9,128]{1,0:T(8,128)}, u32[]{:S(2)}) copy-start(f32[9,128]{1,0:T(8,128)} %constant.9.clone.tw_sin) | copy-start | bytes 13828
  8.7 0.7 %copy-start.8 = (f32[9,128]{1,0:T(8,128)S(1)}, f32[9,128]{1,0:T(8,128)}, u32[]{:S(2)}) copy-start(f32[9,128]{1,0:T(8,128)} %constant.8.clone.tw_cos) | copy-start | bytes 13828

commit v2 on v1

--- a/solution.py
+++ b/solution.py
@@ -41,8 +41,9 @@
 
 def kernel(
     sectors, bands,
-    tracer, wind_east, wind_north, kappa, cutoff, partner, tw_cos, tw_sin, fwd, inv,
+    tracer_h, wind_east_h, wind_north_h, kappa_h, cutoff_h, partner_h, tw_cos_h, tw_sin_h, fwd_h, inv_h,
     filtered, balanced,
+    tracer, wind_east, wind_north, kappa, cutoff, partner, tw_cos, tw_sin, fwd, inv, load_s,
     col_send, col_recv, edge_send, edge_recv, spread, send_b, recv_b, coupling, scaled, ping, pong,
     halo_ss, halo_rs, a_ss, a_rs, b_ss, b_rs,
 ):
@@ -62,6 +63,12 @@
     def band(offset):
         return lax.rem(lat + (offset % bands), bands)
 
+    held = (tracer_h, partner_h, wind_east_h, wind_north_h, kappa_h, cutoff_h, tw_cos_h, tw_sin_h, fwd_h, inv_h)
+    near = (tracer, partner, wind_east, wind_north, kappa, cutoff, tw_cos, tw_sin, fwd, inv)
+    loads = [pltpu.make_async_copy(h, v, load_s.at[i]) for i, (h, v) in enumerate(zip(held, near))]
+    for load in loads:
+        load.start()
+
     barrier = pltpu.get_barrier_semaphore()
     for t in range(1, sectors):
         pl.semaphore_signal(barrier, inc=1, device_id=(lat, sector(t)), device_id_type=pl.DeviceIdType.MESH)
@@ -69,6 +76,8 @@
         pl.semaphore_signal(barrier, inc=1, device_id=(band(t), lon), device_id_type=pl.DeviceIdType.MESH)
     pl.semaphore_wait(barrier, sectors + 1)
 
+    loads[0].wait()
+    loads[1].wait()
     lane2 = lax.broadcasted_iota(jnp.int32, (rows, width), 1)
     row2 = lax.broadcasted_iota(jnp.int32, (rows, width), 0)
     diagonal = lax.broadcasted_iota(jnp.int32, (groups, 8, width), 0) == lax.broadcasted_iota(
@@ -129,6 +138,8 @@
         )
 
     copies = post(0, tracer)
+    for load in loads[2:]:
+        load.wait()
     for l in range(lev):
         coupling[l] = kappa[l] / (1.0 + 4.0 * kappa[l])
     for copy in copies:
@@ -262,12 +273,16 @@
         turns = SWEEPS + 1
         block = pltpu.VMEM((lev, rows, width), jnp.float32)
         vmem = pl.BlockSpec(memory_space=pltpu.VMEM)
+        small = (cutoff.reshape(1, -1), partner.reshape(sectors, width), *tables(sectors, width))
         return pl.pallas_call(
             functools.partial(kernel, sectors, bands),
             out_shape=[jax.ShapeDtypeStruct(tracer.shape, jnp.float32)] * 2,
-            in_specs=[vmem] * 10,
+            in_specs=[pl.BlockSpec(memory_space=pltpu.HBM)] * 10,
             out_specs=[vmem] * 2,
             scratch_shapes=[
+                block, block, block, block,
+                *[pltpu.VMEM(a.shape, a.dtype) for a in small],
+                pltpu.SemaphoreType.DMA((10,)),
                 pltpu.VMEM((turns, 2, 8, width), jnp.float32),
                 pltpu.VMEM((turns, 2, 8, width), jnp.float32),
                 pltpu.VMEM((turns, 2 * lev, width), jnp.float32),
@@ -284,12 +299,10 @@
                 pltpu.SemaphoreType.DMA((sectors,)),
             ],
             compiler_params=pltpu.CompilerParams(
-                collective_id=0, has_side_effects=True, vmem_limit_bytes=32 * 1024 * 1024
+                collective_id=0, has_side_effects=True, vmem_limit_bytes=60 * 1024 * 1024
             ),
         )(
-            tracer, wind_east, wind_north, kappa,
-            cutoff.reshape(1, -1), partner.reshape(sectors, width),
-            *tables(sectors, width),
+            tracer, wind_east, wind_north, kappa, *small,
         )
 
     spec = P(None, "lat", "lon")

time: 51.3 us -> 44.5 us (0.87)
  local copies, waits for them, and re-layouts: 10.3 us -> 2.72 us
  Pallas kernels: 39.9 us -> 41 us
    unnamed x22 -> x4, local copies, waits for them, and re-layouts: 10.3 us -> 2.72 us
    pallas_call x1, Pallas kernels: 39.9 us -> 41 us  [per_device(): pl.pallas_call(functools.partial(kernel, sectors, bands), out_shape=[jax....]
where the time goes in v2:
time: 44.5 us; the launch traced here: 44.3 us
  Pallas kernels  41 us (92%)
  local copies, waits for them, and re-layouts  2.72 us (6%)
  between operations  0.65 us (1%)
    pallas_call x1, Pallas kernels, per_device(): pl.pallas_call(functools.partial(kernel, sectors, bands), out_shape=[jax....  41 us
    unnamed x4, local copies, waits for them, and re-layouts  2.72 us

profile of v2, /device:TPU:0, one launch (start us, length us, event | category | flops | bytes accessed | tf_op | source)
XLA Modules:
  0.0 44.3 jit_solution(7188076857973413451)
XLA Ops:
  0.6 41.0 %shard_map.113 = (f32[4,256,128]{2,1,0:T(8,128)}, f32[4,256,128]{2,1,0:T(8,128)}) custom-call(f32[4,256,128]{2,1,0:T(8,128)} %tracer_h.1, f32[4,256,128]{2,1,0:T(8,128)} %wind_east_h.1, f32[4,256,128]{2,1,0:T(8,128)} %wind_north_h.1, f32[4,256,128]{2,1,0:T(8,128)} %kappa_h.1, s32[1,128]{1,0:T(1,128)} %bitcast.3, s32[16,128]{1,0:T(8,128)} %bitcast.2, ...), custom_call_target="tpu_custom_call" | custom-call | tf_op jit(solution)/shard_map/pallas_call | solution.py:277
  41.6 0.0 copy-start
  41.6 1.9 %copy.14 = f32[4,256,128]{2,1,0:T(8,128)} copy(f32[4,256,128]{2,1,0:T(8,128)} %get-tuple-element.4) | data formatting | bytes 1048576
  43.5 0.0 copy-done
  43.5 0.8 %copy.15 = f32[4,256,128]{2,1,0:T(8,128)} copy(f32[4,256,128]{2,1,0:T(8,128)S(1)} %copy-done) | data formatting | bytes 1048576
Async XLA Ops:
  41.6 1.9 %copy-start = (f32[4,256,128]{2,1,0:T(8,128)S(1)}, f32[4,256,128]{2,1,0:T(8,128)}, u32[]{:S(2)}) copy-start(f32[4,256,128]{2,1,0:T(8,128)} %get-tuple-element.5) | copy-start | bytes 1572868

commit v3 on v2

--- a/solution.py
+++ b/solution.py
@@ -72,9 +72,10 @@
     barrier = pltpu.get_barrier_semaphore()
     for t in range(1, sectors):
         pl.semaphore_signal(barrier, inc=1, device_id=(lat, sector(t)), device_id_type=pl.DeviceIdType.MESH)
-    for t in (1, -1):
+    beside = (1,) if bands == 2 else (1, -1)
+    for t in beside:
         pl.semaphore_signal(barrier, inc=1, device_id=(band(t), lon), device_id_type=pl.DeviceIdType.MESH)
-    pl.semaphore_wait(barrier, sectors + 1)
+    pl.semaphore_wait(barrier, sectors - 1 + len(beside))
 
     loads[0].wait()
     loads[1].wait()
@@ -87,23 +88,38 @@
     reach = jnp.where(reach < 0, reach + sectors * width, reach)
     pick = jnp.where(
         lax.broadcasted_iota(jnp.int32, (2 * width, width), 0) == reach, 1.0, 0.0
-    ).astype(jnp.float32)
-
-    def post(turn, field):
+    ).astype(jnp.bfloat16)
+    lane8 = lax.broadcasted_iota(jnp.int32, (8, width), 1)
+    row8 = lax.broadcasted_iota(jnp.int32, (8, width), 0)
+    inner = lax.rem(lane8, per)
+    level_of = lax.broadcasted_iota(jnp.int32, (lev, width), 0) * per
+    place = lax.broadcasted_iota(jnp.int32, (lev, width), 1)
+    head, tail = place == level_of, place == level_of + per - 1
+
+    def column(field, at):
         whole = field[...].reshape(groups, 8, width)
-        col_send[turn, 0] = jnp.sum(jnp.where(diagonal, whole[:, :, width - 1 : width], 0.0), axis=0)
-        col_send[turn, 1] = jnp.sum(jnp.where(diagonal, whole[:, :, 0:1], 0.0), axis=0)
-        for l in range(lev):
-            edge_send[turn, l : l + 1, :] = field[l, 0:1, :]
-            edge_send[turn, lev + l : lev + l + 1, :] = field[l, rows - 1 : rows, :]
+        return jnp.sum(jnp.where(diagonal, whole[:, :, at : at + 1], 0.0), axis=0)
+
+    def border(field, depth):
+        return jnp.concatenate(
+            [field[l, depth : depth + 1, :] for l in range(lev)]
+            + [field[l, rows - 1 - depth : rows - depth, :] for l in range(lev)],
+            axis=0,
+        )
+
+    def post(turn, edge, first_column, last_column):
+        edge_send[turn] = edge
+        col_send[turn, 0] = last_column
+        col_send[turn, 1] = first_column
         plan = [
             (edge_send.at[turn], edge_recv.at[turn, 0], (lat, sector(-half))),
             (edge_send.at[turn], edge_recv.at[turn, 1], (lat, sector(-half - 1))),
             (edge_send.at[turn], edge_recv.at[turn, 2], (band(1), lon)),
-            (edge_send.at[turn], edge_recv.at[turn, 3], (band(-1), lon)),
             (col_send.at[turn, 0], col_recv.at[turn, 0], (lat, sector(1))),
             (col_send.at[turn, 1], col_recv.at[turn, 1], (lat, sector(-1))),
         ]
+        if bands != 2:
+            plan.append((edge_send.at[turn], edge_recv.at[turn, 3], (band(-1), lon)))
         copies = []
         for i, (src, dst, device) in enumerate(plan):
             copy = pltpu.make_async_remote_copy(
@@ -114,16 +130,40 @@
             copies.append(copy)
         return copies
 
-    def sides(turn):
-        across = jnp.dot(
-            jnp.concatenate([edge_recv[turn, 0], edge_recv[turn, 1]], axis=1), pick,
-            precision=HIGHEST, preferred_element_type=jnp.float32,
-        )
+    def outer(turn):
+        x = jnp.concatenate([edge_recv[turn, 0], edge_recv[turn, 1]], axis=1)
+        high = x.astype(jnp.bfloat16).astype(jnp.float32)
+        rest = x - high
+        middle = rest.astype(jnp.bfloat16).astype(jnp.float32)
+        parts = jnp.concatenate([high, middle, rest - middle], axis=0).astype(jnp.bfloat16)
+        found = jnp.dot(parts, pick, preferred_element_type=jnp.float32)
+        n = 2 * lev
+        across = found[:n] + found[n : 2 * n] + found[2 * n :]
         top = jnp.where(lat == 0, across[:lev], edge_recv[turn, 2, lev:])
-        bottom = jnp.where(lat == bands - 1, across[lev:], edge_recv[turn, 3, :lev])
+        bottom = jnp.where(lat == bands - 1, across[lev:], edge_recv[turn, 2 if bands == 2 else 3, :lev])
+        return top, bottom
+
+    def sides(turn, top, bottom):
         west = jnp.sum(jnp.where(diagonal, col_recv[turn, 0][None], 0.0), axis=2, keepdims=True)
         east = jnp.sum(jnp.where(diagonal, col_recv[turn, 1][None], 0.0), axis=2, keepdims=True)
         return top, bottom, west, east
+
+    def along(packed, top, bottom, at):
+        above = jnp.sum(jnp.where(head, top[:, at : at + 1], 0.0), axis=0, keepdims=True)
+        below = jnp.sum(jnp.where(tail, bottom[:, at : at + 1], 0.0), axis=0, keepdims=True)
+        up, down = pltpu.roll(packed, 1, 0), pltpu.roll(packed, 7, 0)
+        up = jnp.where(row8 == 0, jnp.where(inner == 0, above, pltpu.roll(up, 1, 1)), up)
+        down = jnp.where(row8 == 7, jnp.where(inner == per - 1, below, pltpu.roll(down, width - 1, 1)), down)
+        return up + down
+
+    def ends(packed):
+        return jnp.concatenate(
+            [
+                jnp.sum(jnp.where(head, packed[0:1], 0.0), axis=1, keepdims=True),
+                jnp.sum(jnp.where(tail, packed[7:8], 0.0), axis=1, keepdims=True),
+            ],
+            axis=0,
+        )
 
     def around(field, l, edges):
         top, bottom, west, east = edges
@@ -137,14 +177,14 @@
             jnp.where(row2 == rows - 1, bottom[l : l + 1], pltpu.roll(x, rows - 1, 0)),
         )
 
-    copies = post(0, tracer)
+    copies = post(0, border(tracer, 0), column(tracer, 0), column(tracer, width - 1))
     for load in loads[2:]:
         load.wait()
     for l in range(lev):
         coupling[l] = kappa[l] / (1.0 + 4.0 * kappa[l])
     for copy in copies:
         copy.wait()
-    edges = sides(0)
+    edges = sides(0, *outer(0))
     for l in range(lev):
         w, e, u, d = around(tracer, l, edges)
         filtered[l] = tracer[l] - COURANT * 0.5 * (wind_east[l] * (e - w) + wind_north[l] * (d - u))
@@ -249,16 +289,34 @@
     def _():
         restore(rows - pole)
 
+    edge, first_column, last_column = border(filtered, 0), column(filtered, 0), column(filtered, width - 1)
+    copies = post(1, edge, first_column, last_column)
+    for l in range(lev):
+        scaled[l] = filtered[l] / (1.0 + 4.0 * kappa[l])
+    fixed = [(border(a, 0), column(a, 0), column(a, width - 1)) for a in (scaled, coupling)]
     chain = [filtered, ping, pong, ping, balanced]
     for sweep in range(SWEEPS):
-        source, target = chain[sweep], chain[sweep + 1]
-        copies = post(1 + sweep, source)
-        if sweep == 0:
-            for l in range(lev):
-                scaled[l] = filtered[l] / (1.0 + 4.0 * kappa[l])
+        turn, source, target = 1 + sweep, chain[sweep], chain[sweep + 1]
+        if sweep < SWEEPS - 1:
+            second, second_first, second_last = border(source, 1), column(source, 1), column(source, width - 2)
         for copy in copies:
             copy.wait()
-        edges = sides(1 + sweep)
+        top, bottom = outer(turn)
+        if sweep < SWEEPS - 1:
+            west, east = col_recv[turn, 0], col_recv[turn, 1]
+            around_edge = (
+                jnp.where(lane8 == 0, ends(west), pltpu.roll(edge, 1, 1))
+                + jnp.where(lane8 == width - 1, ends(east), pltpu.roll(edge, width - 1, 1))
+                + jnp.concatenate([top, bottom], axis=0)
+                + second
+            )
+            around_first = west + second_first + along(first_column, top, bottom, 0)
+            around_last = east + second_last + along(last_column, top, bottom, width - 1)
+            edge, first_column, last_column = [
+                a + b * c for a, b, c in zip(*fixed, (around_edge, around_first, around_last))
+            ]
+            copies = post(turn + 1, edge, first_column, last_column)
+        edges = sides(turn, top, bottom)
         for l in range(lev):
             w, e, u, d = around(source, l, edges)
             target[l] = scaled[l] + coupling[l] * (w + e + u + d)
@@ -299,10 +357,10 @@
                 pltpu.SemaphoreType.DMA((sectors,)),
             ],
             compiler_params=pltpu.CompilerParams(
-                collective_id=0, has_side_effects=True, vmem_limit_bytes=60 * 1024 * 1024
+                collective_id=0, has_side_effects=True, vmem_limit_bytes=32 * 1024 * 1024
             ),
         )(
-            tracer, wind_east, wind_north, kappa, *small,
+            *[pltpu.with_memory_space_constraint(jnp.asarray(a), pltpu.HBM) for a in (tracer, wind_east, wind_north, kappa, *small)]
         )
 
     spec = P(None, "lat", "lon")

time: 44.5 us -> 40.2 us (0.903)
  Pallas kernels: 41 us -> 37.8 us
  local copies, waits for them, and re-layouts: 2.72 us -> 1.59 us
    pallas_call x1, Pallas kernels: 41 us -> 37.8 us  [per_device(): pl.pallas_call(functools.partial(kernel, sectors, bands), out_shape=[jax....]
    unnamed x4 -> x2, local copies, waits for them, and re-layouts: 2.72 us -> 1.59 us
where the time goes in v3:
time: 40.2 us; the launch traced here: 40 us
  Pallas kernels  37.8 us (94%)
  local copies, waits for them, and re-layouts  1.59 us (4%)
  between operations  0.64 us (2%)
    pallas_call x1, Pallas kernels, per_device(): pl.pallas_call(functools.partial(kernel, sectors, bands), out_shape=[jax....  37.8 us
    unnamed x2, local copies, waits for them, and re-layouts  1.59 us

profile of v3, /device:TPU:0, one launch (start us, length us, event | category | flops | bytes accessed | tf_op | source)
XLA Modules:
  0.0 40.0 jit_solution(16288840348697795030)
XLA Ops:
  0.6 37.8 %shard_map.113 = (f32[4,256,128]{2,1,0:T(8,128)S(1)}, f32[4,256,128]{2,1,0:T(8,128)S(1)}) custom-call(f32[4,256,128]{2,1,0:T(8,128)} %tracer_h.1, f32[4,256,128]{2,1,0:T(8,128)} %wind_east_h.1, f32[4,256,128]{2,1,0:T(8,128)} %wind_north_h.1, f32[4,256,128]{2,1,0:T(8,128)} %kappa_h.1, s32[1,128]{1,0:T(1,128)} %bitcast.3, s32[16,128]{1,0:T(8,128)} %bitcast.2, ...), custom_call_target="tpu_custom_call" | custom-call | tf_op jit(solution)/shard_map/pallas_call | solution.py:335
  38.5 0.8 %copy.14 = f32[4,256,128]{2,1,0:T(8,128)} copy(f32[4,256,128]{2,1,0:T(8,128)S(1)} %get-tuple-element.4) | data formatting | bytes 1048576
  39.2 0.8 %copy.15 = f32[4,256,128]{2,1,0:T(8,128)} copy(f32[4,256,128]{2,1,0:T(8,128)S(1)} %get-tuple-element.5) | data formatting | bytes 1048576

commit v4 on v3

--- a/solution.py
+++ b/solution.py
@@ -44,7 +44,7 @@
     tracer_h, wind_east_h, wind_north_h, kappa_h, cutoff_h, partner_h, tw_cos_h, tw_sin_h, fwd_h, inv_h,
     filtered, balanced,
     tracer, wind_east, wind_north, kappa, cutoff, partner, tw_cos, tw_sin, fwd, inv, load_s,
-    col_send, col_recv, edge_send, edge_recv, spread, send_b, recv_b, coupling, scaled, ping, pong,
+    col_send, col_recv, edge_send, edge_recv, stage, spread, send_b, recv_b, coupling, scaled, ping, pong,
     halo_ss, halo_rs, a_ss, a_rs, b_ss, b_rs,
 ):
     lev, rows, width = tracer.shape
@@ -181,31 +181,61 @@
     for load in loads[2:]:
         load.wait()
     for l in range(lev):
-        coupling[l] = kappa[l] / (1.0 + 4.0 * kappa[l])
+        inverse = 1.0 / (1.0 + 4.0 * kappa[l])
+        scaled[l] = inverse
+        coupling[l] = kappa[l] * inverse
+    last = lat == bands - 1
+    base = pl.multiple_of(jnp.where(last, rows - pole, 0), 8)
+    before = jnp.where(last, rows - pole - 1, 0)
+    after = jnp.where(last, rows - 1, pole)
+    offset = jnp.where(last, (rows - pole) // 8, 0)
+    shape = (pole // 8, 8, width)
+    lane_p = lax.broadcasted_iota(jnp.int32, (pole, width), 1)
+    row_p = lax.broadcasted_iota(jnp.int32, (pole, width), 0)
     for copy in copies:
         copy.wait()
-    edges = sides(0, *outer(0))
+    top, bottom = outer(0)
+
+    def spoke(packed, l):
+        mine = lax.broadcasted_iota(jnp.int32, shape, 0) + (per * l + offset) == lax.broadcasted_iota(
+            jnp.int32, shape, 2
+        )
+        value = jnp.sum(jnp.where(mine, packed[None], 0.0), axis=2, keepdims=True)
+        return jnp.broadcast_to(value, shape).reshape(pole, width)
+
+    def to_share(l, q):
+        device = l * slices + q
+        return pltpu.make_async_remote_copy(
+            src_ref=stage.at[l, pl.ds(q * share, share), :], dst_ref=spread.at[lon],
+            send_sem=a_ss.at[device], recv_sem=a_rs.at[lon],
+            device_id=(lat, device), device_id_type=pl.DeviceIdType.MESH,
+        )
+
+    for l in range(lev):
+        x = tracer[l, pl.ds(base, pole), :]
+        w = jnp.where(lane_p == 0, spoke(col_recv[0, 0], l), pltpu.roll(x, 1, 1))
+        e = jnp.where(lane_p == width - 1, spoke(col_recv[0, 1], l), pltpu.roll(x, width - 1, 1))
+        above = jnp.where(last, tracer[l, pl.ds(before, 1), :], top[l : l + 1])
+        below = jnp.where(last, bottom[l : l + 1], tracer[l, pl.ds(after, 1), :])
+        u = jnp.where(row_p == 0, above, pltpu.roll(x, 1, 0))
+        d = jnp.where(row_p == pole - 1, below, pltpu.roll(x, pole - 1, 0))
+        stage[l] = x - COURANT * 0.5 * (
+            wind_east[l, pl.ds(base, pole), :] * (e - w) + wind_north[l, pl.ds(base, pole), :] * (d - u)
+        )
+        for q in range(slices):
+            @pl.when(lon != l * slices + q)
+            def _(l=l, q=q):
+                to_share(l, q).start()
+
+            @pl.when(lon == l * slices + q)
+            def _(l=l, q=q):
+                spread[l * slices + q] = stage[l, q * share : (q + 1) * share, :]
+
+    edges = sides(0, top, bottom)
     for l in range(lev):
         w, e, u, d = around(tracer, l, edges)
         filtered[l] = tracer[l] - COURANT * 0.5 * (wind_east[l] * (e - w) + wind_north[l] * (d - u))
-
-    base = jnp.where(lat == bands - 1, rows - pole, 0)
-
-    def part(device):
-        return lax.div(device, slices), pl.ds(pl.multiple_of(base + lax.rem(device, slices) * share, 8), share)
-
-    copies = []
-    for t in range(1, sectors):
-        level, span = part(sector(t))
-        copy = pltpu.make_async_remote_copy(
-            src_ref=filtered.at[level, span, :], dst_ref=spread.at[lon],
-            send_sem=a_ss.at[t], recv_sem=a_rs.at[t],
-            device_id=(lat, sector(t)), device_id_type=pl.DeviceIdType.MESH,
-        )
-        copy.start()
-        copies.append(copy)
-    level, span = part(lon)
-    spread[lon] = filtered[level, span, :]
+    fixed = [(border(a, 0), column(a, 0), column(a, width - 1)) for a in (scaled, coupling)]
 
     first = jnp.where(lat == bands - 1, pole, 0) + lax.rem(lon, slices) * share
     spot = lax.broadcasted_iota(jnp.int32, (share, 2 * pole), 0) + first
@@ -219,8 +249,14 @@
     kept = 2 * KMAX // sectors
     slot = lax.broadcasted_iota(jnp.int32, (share, 2 * kept), 1)
     wave = sectors * (jnp.where(slot < kept, slot, slot - kept) - kept // 2)
-    for copy in copies:
-        copy.wait()
+    for device in range(sectors):
+        @pl.when(lon != device)
+        def _(device=device):
+            pltpu.make_async_remote_copy(
+                src_ref=stage.at[device // slices, pl.ds(device % slices * share, share), :],
+                dst_ref=spread.at[device], send_sem=a_ss.at[device], recv_sem=a_rs.at[device],
+                device_id=(lat, device), device_id_type=pl.DeviceIdType.MESH,
+            ).wait()
 
     def circle(d, k):
         angle = 2.0 * math.pi * ((d * k) % sectors) / sectors
@@ -273,8 +309,30 @@
         copy.start()
         copies.append(copy)
     recv_b[lon] = send_b[lon]
+    plain = border(filtered, 0), column(filtered, 0), column(filtered, width - 1)
+    polar = (lat == 0) | last
     for copy in copies:
         copy.wait()
+
+    cells = recv_b[...].reshape(lev * pole // 8, 8, width)
+    order = lax.broadcasted_iota(jnp.int32, cells.shape, 0)
+    order = lax.div(order, pole // 8) * per + offset + lax.rem(order, pole // 8)
+    mine = order == lax.broadcasted_iota(jnp.int32, cells.shape, 2)
+    step = lax.rem(lane8, per) - offset
+    fresh = (step >= 0) & (step < pole // 8) & polar
+
+    def renewed(old, at):
+        return jnp.where(fresh, jnp.sum(jnp.where(mine, cells[:, :, at : at + 1], 0.0), axis=0), old)
+
+    rim = jnp.concatenate(
+        [recv_b[l * slices, 0:1, :] for l in range(lev)]
+        + [recv_b[l * slices + slices - 1, share - 1 : share, :] for l in range(lev)],
+        axis=0,
+    )
+    edge = jnp.where(((row8 < lev) & (lat == 0)) | ((row8 >= lev) & last), rim, plain[0])
+    first_column, last_column = renewed(plain[1], 0), renewed(plain[2], width - 1)
+    copies = post(1, edge, first_column, last_column)
+    fixed[0] = tuple(a * b for a, b in zip(fixed[0], (edge, first_column, last_column)))
 
     def restore(start):
         for l in range(lev):
@@ -289,11 +347,8 @@
     def _():
         restore(rows - pole)
 
-    edge, first_column, last_column = border(filtered, 0), column(filtered, 0), column(filtered, width - 1)
-    copies = post(1, edge, first_column, last_column)
     for l in range(lev):
-        scaled[l] = filtered[l] / (1.0 + 4.0 * kappa[l])
-    fixed = [(border(a, 0), column(a, 0), column(a, width - 1)) for a in (scaled, coupling)]
+        scaled[l] = filtered[l] * scaled[l]
     chain = [filtered, ping, pong, ping, balanced]
     for sweep in range(SWEEPS):
         turn, source, target = 1 + sweep, chain[sweep], chain[sweep + 1]
@@ -345,6 +400,7 @@
                 pltpu.VMEM((turns, 2, 8, width), jnp.float32),
                 pltpu.VMEM((turns, 2 * lev, width), jnp.float32),
                 pltpu.VMEM((turns, 4, 2 * lev, width), jnp.float32),
+                pltpu.VMEM((lev, cutoff.shape[0] // 2, width), jnp.float32),
                 pltpu.VMEM((sectors, share, width), jnp.float32),
                 pltpu.VMEM((sectors, share, width), jnp.float32),
                 pltpu.VMEM((sectors, share, width), jnp.float32),

time: 40.2 us -> 39.4 us (0.980)
  Pallas kernels: 37.8 us -> 37 us
    pallas_call x1, Pallas kernels: 37.8 us -> 37 us  [per_device(): pl.pallas_call(functools.partial(kernel, sectors, bands), out_shape=[jax....]
where the time goes in v4:
time: 39.4 us; the launch traced here: 39.3 us
  Pallas kernels  37 us (94%)
  local copies, waits for them, and re-layouts  1.59 us (4%)
  between operations  0.64 us (2%)
    pallas_call x1, Pallas kernels, per_device(): pl.pallas_call(functools.partial(kernel, sectors, bands), out_shape=[jax....  37 us
    unnamed x2, local copies, waits for them, and re-layouts  1.59 us

profile of v4, /device:TPU:0, one launch (start us, length us, event | category | flops | bytes accessed | tf_op | source)
XLA Modules:
  0.0 39.3 jit_solution(14633152419952883735)
XLA Ops:
  0.6 37.0 %shard_map.113 = (f32[4,256,128]{2,1,0:T(8,128)S(1)}, f32[4,256,128]{2,1,0:T(8,128)S(1)}) custom-call(f32[4,256,128]{2,1,0:T(8,128)} %tracer_h.1, f32[4,256,128]{2,1,0:T(8,128)} %wind_east_h.1, f32[4,256,128]{2,1,0:T(8,128)} %wind_north_h.1, f32[4,256,128]{2,1,0:T(8,128)} %kappa_h.1, s32[1,128]{1,0:T(1,128)} %bitcast.3, s32[16,128]{1,0:T(8,128)} %bitcast.2, ...), custom_call_target="tpu_custom_call" | custom-call | tf_op jit(solution)/shard_map/pallas_call | solution.py:390
  37.7 0.8 %copy.14 = f32[4,256,128]{2,1,0:T(8,128)} copy(f32[4,256,128]{2,1,0:T(8,128)S(1)} %get-tuple-element.4) | data formatting | bytes 1048576
  38.5 0.8 %copy.15 = f32[4,256,128]{2,1,0:T(8,128)} copy(f32[4,256,128]{2,1,0:T(8,128)S(1)} %get-tuple-element.5) | data formatting | bytes 1048576

commit v5 on v4

--- a/solution.py
+++ b/solution.py
@@ -95,6 +95,8 @@
     level_of = lax.broadcasted_iota(jnp.int32, (lev, width), 0) * per
     place = lax.broadcasted_iota(jnp.int32, (lev, width), 1)
     head, tail = place == level_of, place == level_of + per - 1
+
+    sent = []
 
     def column(field, at):
         whole = field[...].reshape(groups, 8, width)
@@ -128,6 +130,7 @@
             )
             copy.start()
             copies.append(copy)
+        sent.extend(copies)
         return copies
 
     def outer(turn):
@@ -193,7 +196,7 @@
     lane_p = lax.broadcasted_iota(jnp.int32, (pole, width), 1)
     row_p = lax.broadcasted_iota(jnp.int32, (pole, width), 0)
     for copy in copies:
-        copy.wait()
+        copy.wait_recv()
     top, bottom = outer(0)
 
     def spoke(packed, l):
@@ -202,14 +205,6 @@
         )
         value = jnp.sum(jnp.where(mine, packed[None], 0.0), axis=2, keepdims=True)
         return jnp.broadcast_to(value, shape).reshape(pole, width)
-
-    def to_share(l, q):
-        device = l * slices + q
-        return pltpu.make_async_remote_copy(
-            src_ref=stage.at[l, pl.ds(q * share, share), :], dst_ref=spread.at[lon],
-            send_sem=a_ss.at[device], recv_sem=a_rs.at[lon],
-            device_id=(lat, device), device_id_type=pl.DeviceIdType.MESH,
-        )
 
     for l in range(lev):
         x = tracer[l, pl.ds(base, pole), :]
@@ -222,14 +217,20 @@
         stage[l] = x - COURANT * 0.5 * (
             wind_east[l, pl.ds(base, pole), :] * (e - w) + wind_north[l, pl.ds(base, pole), :] * (d - u)
         )
-        for q in range(slices):
-            @pl.when(lon != l * slices + q)
-            def _(l=l, q=q):
-                to_share(l, q).start()
-
-            @pl.when(lon == l * slices + q)
-            def _(l=l, q=q):
-                spread[l * slices + q] = stage[l, q * share : (q + 1) * share, :]
+    order_out = sorted(range(1, sectors), key=lambda t: abs(t - half))
+    rows_out = []
+    for t in order_out:
+        device = sector(t)
+        span = pl.ds(pl.multiple_of(lax.rem(device, slices) * share, 8), share)
+        copy = pltpu.make_async_remote_copy(
+            src_ref=stage.at[lax.div(device, slices), span, :], dst_ref=spread.at[lon],
+            send_sem=a_ss.at[t], recv_sem=a_rs.at[t],
+            device_id=(lat, device), device_id_type=pl.DeviceIdType.MESH,
+        )
+        copy.start()
+        rows_out.append(copy)
+    sent.extend(rows_out)
+    spread[lon] = stage[lax.div(lon, slices), pl.ds(pl.multiple_of(lax.rem(lon, slices) * share, 8), share), :]
 
     edges = sides(0, top, bottom)
     for l in range(lev):
@@ -249,14 +250,8 @@
     kept = 2 * KMAX // sectors
     slot = lax.broadcasted_iota(jnp.int32, (share, 2 * kept), 1)
     wave = sectors * (jnp.where(slot < kept, slot, slot - kept) - kept // 2)
-    for device in range(sectors):
-        @pl.when(lon != device)
-        def _(device=device):
-            pltpu.make_async_remote_copy(
-                src_ref=stage.at[device // slices, pl.ds(device % slices * share, share), :],
-                dst_ref=spread.at[device], send_sem=a_ss.at[device], recv_sem=a_rs.at[device],
-                device_id=(lat, device), device_id_type=pl.DeviceIdType.MESH,
-            ).wait()
+    for copy in rows_out:
+        copy.wait_recv()
 
     def circle(d, k):
         angle = 2.0 * math.pi * ((d * k) % sectors) / sectors
@@ -300,7 +295,7 @@
             send_b[sectors - d] = p + q
 
     copies = []
-    for t in range(1, sectors):
+    for t in order_out:
         copy = pltpu.make_async_remote_copy(
             src_ref=send_b.at[sector(t)], dst_ref=recv_b.at[lon],
             send_sem=b_ss.at[t], recv_sem=b_rs.at[t],
@@ -308,11 +303,12 @@
         )
         copy.start()
         copies.append(copy)
+    sent.extend(copies)
     recv_b[lon] = send_b[lon]
     plain = border(filtered, 0), column(filtered, 0), column(filtered, width - 1)
     polar = (lat == 0) | last
     for copy in copies:
-        copy.wait()
+        copy.wait_recv()
 
     cells = recv_b[...].reshape(lev * pole // 8, 8, width)
     order = lax.broadcasted_iota(jnp.int32, cells.shape, 0)
@@ -355,7 +351,7 @@
         if sweep < SWEEPS - 1:
             second, second_first, second_last = border(source, 1), column(source, 1), column(source, width - 2)
         for copy in copies:
-            copy.wait()
+            copy.wait_recv()
         top, bottom = outer(turn)
         if sweep < SWEEPS - 1:
             west, east = col_recv[turn, 0], col_recv[turn, 1]
@@ -375,6 +371,8 @@
         for l in range(lev):
             w, e, u, d = around(source, l, edges)
             target[l] = scaled[l] + coupling[l] * (w + e + u + d)
+    for copy in sent:
+        copy.wait_send()
 
 
 def solution(mesh):

time: 39.4 us -> 40.6 us (1.030)
  Pallas kernels: 37 us -> 38.2 us
    pallas_call x1, Pallas kernels: 37 us -> 38.2 us  [per_device(): pl.pallas_call(functools.partial(kernel, sectors, bands), out_shape=[jax....]
where the time goes in v5:
time: 40.6 us; the launch traced here: 40.4 us
  Pallas kernels  38.2 us (94%)
  local copies, waits for them, and re-layouts  1.59 us (4%)
  between operations  0.64 us (2%)
    pallas_call x1, Pallas kernels, per_device(): pl.pallas_call(functools.partial(kernel, sectors, bands), out_shape=[jax....  38.2 us
    unnamed x2, local copies, waits for them, and re-layouts  1.59 us

profile of v5, /device:TPU:0, one launch (start us, length us, event | category | flops | bytes accessed | tf_op | source)
XLA Modules:
  0.0 40.4 jit_solution(3448383856413840107)
XLA Ops:
  0.6 38.2 %shard_map.113 = (f32[4,256,128]{2,1,0:T(8,128)S(1)}, f32[4,256,128]{2,1,0:T(8,128)S(1)}) custom-call(f32[4,256,128]{2,1,0:T(8,128)} %tracer_h.1, f32[4,256,128]{2,1,0:T(8,128)} %wind_east_h.1, f32[4,256,128]{2,1,0:T(8,128)} %wind_north_h.1, f32[4,256,128]{2,1,0:T(8,128)} %kappa_h.1, s32[1,128]{1,0:T(1,128)} %bitcast.3, s32[16,128]{1,0:T(8,128)} %bitcast.2, ...), custom_call_target="tpu_custom_call" | custom-call | tf_op jit(solution)/shard_map/pallas_call | solution.py:388
  38.8 0.8 %copy.14 = f32[4,256,128]{2,1,0:T(8,128)} copy(f32[4,256,128]{2,1,0:T(8,128)S(1)} %get-tuple-element.4) | data formatting | bytes 1048576
  39.6 0.8 %copy.15 = f32[4,256,128]{2,1,0:T(8,128)} copy(f32[4,256,128]{2,1,0:T(8,128)S(1)} %get-tuple-element.5) | data formatting | bytes 1048576

commit v6 on v4

--- a/solution.py
+++ b/solution.py
@@ -95,6 +95,8 @@
     level_of = lax.broadcasted_iota(jnp.int32, (lev, width), 0) * per
     place = lax.broadcasted_iota(jnp.int32, (lev, width), 1)
     head, tail = place == level_of, place == level_of + per - 1
+
+    sent = []
 
     def column(field, at):
         whole = field[...].reshape(groups, 8, width)
@@ -128,6 +130,7 @@
             )
             copy.start()
             copies.append(copy)
+        sent.extend(copies)
         return copies
 
     def outer(turn):
@@ -193,7 +196,7 @@
     lane_p = lax.broadcasted_iota(jnp.int32, (pole, width), 1)
     row_p = lax.broadcasted_iota(jnp.int32, (pole, width), 0)
     for copy in copies:
-        copy.wait()
+        copy.wait_recv()
     top, bottom = outer(0)
 
     def spoke(packed, l):
@@ -308,11 +311,12 @@
         )
         copy.start()
         copies.append(copy)
+    sent.extend(copies)
     recv_b[lon] = send_b[lon]
     plain = border(filtered, 0), column(filtered, 0), column(filtered, width - 1)
     polar = (lat == 0) | last
     for copy in copies:
-        copy.wait()
+        copy.wait_recv()
 
     cells = recv_b[...].reshape(lev * pole // 8, 8, width)
     order = lax.broadcasted_iota(jnp.int32, cells.shape, 0)
@@ -355,7 +359,7 @@
         if sweep < SWEEPS - 1:
             second, second_first, second_last = border(source, 1), column(source, 1), column(source, width - 2)
         for copy in copies:
-            copy.wait()
+            copy.wait_recv()
         top, bottom = outer(turn)
         if sweep < SWEEPS - 1:
             west, east = col_recv[turn, 0], col_recv[turn, 1]
@@ -375,6 +379,8 @@
         for l in range(lev):
             w, e, u, d = around(source, l, edges)
             target[l] = scaled[l] + coupling[l] * (w + e + u + d)
+    for copy in sent:
+        copy.wait_send()
 
 
 def solution(mesh):

time: 39.4 us -> 39.5 us (level)
  no operation moved by 1% of the time
where the time goes in v6:
time: 39.5 us; the launch traced here: 39.3 us
  Pallas kernels  37.1 us (94%)
  local copies, waits for them, and re-layouts  1.59 us (4%)
  between operations  0.64 us (2%)
    pallas_call x1, Pallas kernels, per_device(): pl.pallas_call(functools.partial(kernel, sectors, bands), out_shape=[jax....  37.1 us
    unnamed x2, local copies, waits for them, and re-layouts  1.59 us

profile of v6, /device:TPU:0, one launch (start us, length us, event | category | flops | bytes accessed | tf_op | source)
XLA Modules:
  0.0 39.3 jit_solution(2643825114795747278)
XLA Ops:
  0.6 37.1 %shard_map.113 = (f32[4,256,128]{2,1,0:T(8,128)S(1)}, f32[4,256,128]{2,1,0:T(8,128)S(1)}) custom-call(f32[4,256,128]{2,1,0:T(8,128)} %tracer_h.1, f32[4,256,128]{2,1,0:T(8,128)} %wind_east_h.1, f32[4,256,128]{2,1,0:T(8,128)} %wind_north_h.1, f32[4,256,128]{2,1,0:T(8,128)} %kappa_h.1, s32[1,128]{1,0:T(1,128)} %bitcast.3, s32[16,128]{1,0:T(8,128)} %bitcast.2, ...), custom_call_target="tpu_custom_call" | custom-call | tf_op jit(solution)/shard_map/pallas_call | solution.py:396
  37.7 0.8 %copy.14 = f32[4,256,128]{2,1,0:T(8,128)} copy(f32[4,256,128]{2,1,0:T(8,128)S(1)} %get-tuple-element.4) | data formatting | bytes 1048576
  38.5 0.8 %copy.15 = f32[4,256,128]{2,1,0:T(8,128)} copy(f32[4,256,128]{2,1,0:T(8,128)S(1)} %get-tuple-element.5) | data formatting | bytes 1048576
